TPU v7x, 32 devices: a whole 2x2x4 slice. The times are simulated.
32 devices in a mesh: row: 8 (over y, x, core), col: 4 (over z).
Axes of the slice: x: 2, y: 2, z: 4, core: 2. Of those that a mesh axis runs over, the one named last changes fastest.
Arguments:
- pool: bfloat16 [4096, 128], P(('row', 'col')), may hold values from -6 to 6
- targets: bfloat16 [4096], P(('row', 'col')), may hold values from -15 to 15
- picks: int32 [512], P(('row', 'col')), may hold values from 0 to 127
- inducing: float32 [8192, 128], replicated, may hold values from -6 to 6
- inv_sq_lengths: float32 [128], replicated, may hold values from 0.04 to 0.12
- prec_old: float32 [8192, 8192], P('row', 'col'), may hold values from -1 to 6, as said below
- mean_old: float32 [8192], P('row'), may hold values from -6 to 6
- panel: int32 [1], replicated, may hold values from 0 to 31
Outputs:
- prec_new: float32 [8192, 8192], P('row', 'col')
- mean_new: float32 [8192], P('row')
Inputs may be any that keep to these rules, and one draw needn't show every extreme that they name: `picks`: each entry indexes a row of the dataset block held by the same device as the entry. `prec_old`: symmetric and positive definite.
All inputs are finite; a program needn't handle non-finite values.
Results may differ from a plain program's by a relative error of at most 0.0028.
Values may be sent and summed in bfloat16 or wider, within the bound.
A program may use at most 128 MiB of HBM per device.

v0:
```python
import jax
import jax.numpy as jnp
from jax import lax
from jax.sharding import PartitionSpec as P

M = 8192
PB = 256


RATE = 0.5
EPSILON = 1e-05


def spread(block, axis, source):
    block = jnp.where(lax.axis_index(axis) == source, block, jnp.zeros_like(block))
    return lax.psum(block, axis)


def kernel_block(points, weights, sample_x):
    sample_f = sample_x.astype(jnp.float32)
    point_sq = jnp.sum(points * points * weights, axis=1)
    sample_sq = jnp.sum(sample_f * sample_f * weights, axis=1)
    cross_term = lax.dot_general(
        points * weights, sample_f, (((1,), (1,)), ((), ())), precision=lax.Precision.HIGHEST
    )
    return jnp.exp(-0.5 * (point_sq[:, None] + sample_sq[None, :] - 2.0 * cross_term)).astype(
        jnp.bfloat16
    )


def local_diag(gram_tile, row_base, col_base):
    row_ids = row_base + jnp.arange(gram_tile.shape[0], dtype=jnp.int32)
    col_ids = col_base + jnp.arange(gram_tile.shape[1], dtype=jnp.int32)
    on_diag = row_ids[:, None] == col_ids[None, :]
    return jnp.sum(jnp.where(on_diag, gram_tile, 0.0))


def diag_total(gram_tile, row_base, col_base):
    return lax.psum(local_diag(gram_tile, row_base, col_base), ("row", "col"))


def local(pool, targets, picks, inducing, inv_sq_lengths, prec_old, mean_old, panel):
    n_rows = lax.axis_size("row")
    n_cols = lax.axis_size("col")
    my_row = lax.axis_index("row")
    my_col = lax.axis_index("col")
    tile_rows, tile_cols = prec_old.shape
    batch_count = picks.shape[0] * n_rows * n_cols
    row_base = my_row * tile_rows
    col_base = my_col * tile_cols
    samples = jnp.take(pool, picks, axis=0)
    values = jnp.take(targets, picks, axis=0)
    all_x, all_y = (
        lax.all_gather(samples, ("row", "col"), axis=0, tiled=True),
        lax.all_gather(values, ("row", "col"), axis=0, tiled=True),
    )
    feat_rows = kernel_block(
        lax.dynamic_slice_in_dim(inducing, row_base, tile_rows, 0), inv_sq_lengths, all_x
    )
    feat_cols = kernel_block(
        lax.dynamic_slice_in_dim(inducing, col_base, tile_cols, 0), inv_sq_lengths, all_x
    )
    gram_tile = lax.dot_general(
        feat_rows, feat_cols, (((1,), (1,)), ((), ())), preferred_element_type=jnp.float32
    )
    fit_part = jnp.dot(feat_rows, all_y, preferred_element_type=jnp.float32)
    all_f = all_y.astype(jnp.float32)
    power_sum = jnp.sum(all_f * all_f)
    trace_sum = diag_total(gram_tile, row_base, col_base)
    trace_scale = trace_sum / M
    joined = (1.0 - RATE) * prec_old + RATE * gram_tile / trace_scale
    mean_mid = (1.0 - RATE) * mean_old + RATE * fit_part / jnp.sqrt(
        trace_scale * (power_sum / batch_count + EPSILON)
    )
    panel_start = panel[0] * PB
    owner_row = panel_start // tile_rows
    owner_col = panel_start // tile_cols
    offset_row = panel_start - owner_row * tile_rows
    offset_col = panel_start - owner_col * tile_cols
    zero_index = jnp.zeros((), jnp.int32)
    col_piece = lax.dynamic_slice(joined, (zero_index, offset_col), (tile_rows, PB))
    got_cols = spread(col_piece, "col", owner_col)
    row_piece = lax.dynamic_slice(joined, (offset_row, zero_index), (PB, tile_cols))
    mean_piece = lax.dynamic_slice(mean_mid, (offset_row,), (PB,))
    diag_piece = lax.dynamic_slice(got_cols, (offset_row, zero_index), (PB, PB))
    got_rows, got_mean, got_block = (
        spread(row_piece, "row", owner_row),
        spread(mean_piece, "row", owner_row),
        spread(diag_piece, "row", owner_row),
    )
    factor = jnp.linalg.cholesky(got_block)
    identity = jnp.eye(PB, dtype=jnp.float32)
    inv_factor = lax.linalg.triangular_solve(factor, identity, left_side=True, lower=True)
    wide_rows = lax.dot_general(
        got_cols, inv_factor, (((1,), (1,)), ((), ())), precision=lax.Precision.HIGHEST
    )
    solved_rows = jnp.dot(inv_factor, got_rows, precision=lax.Precision.HIGHEST)
    head_part = jnp.dot(inv_factor, got_mean, precision=lax.Precision.HIGHEST)
    updated = joined - jnp.dot(wide_rows, solved_rows, precision=lax.Precision.HIGHEST)
    in_col = my_col == owner_col
    in_row = my_row == owner_row
    updated = jnp.where(
        in_col, lax.dynamic_update_slice(updated, wide_rows, (zero_index, offset_col)), updated
    )
    updated = jnp.where(
        in_row, lax.dynamic_update_slice(updated, solved_rows, (offset_row, zero_index)), updated
    )
    updated = jnp.where(
        jnp.logical_and(in_row, in_col),
        lax.dynamic_update_slice(updated, factor, (offset_row, offset_col)),
        updated,
    )
    mean_next = mean_mid - jnp.dot(wide_rows, head_part, precision=lax.Precision.HIGHEST)
    mean_next = jnp.where(
        in_row, lax.dynamic_update_slice(mean_next, head_part, (offset_row,)), mean_next
    )
    return (updated, mean_next)


def solution(mesh):
    in_specs = (
        P(("row", "col"), None),
        P(("row", "col")),
        P(("row", "col")),
        P(),
        P(),
        P("row", "col"),
        P("row"),
        P(),
    )
    out_specs = (P("row", "col"), P("row"))
    return jax.shard_map(local, mesh=mesh, in_specs=in_specs, out_specs=out_specs, check_vma=False)
```

profile of v0, /device:TPU:1, one launch (start us, length us, event | category | flops | bytes accessed | tf_op | source)
XLA Modules:
  0.0 394.1 jit_solution(13664006525870587295)
XLA Ops:
  11.3 65.4 %all_gather.6 = bf16[512,128]{1,0:T(8,128)(2,1)S(1)} all-gather(bf16[16,128]{1,0:T(8,128)(2,1)S(1)} %broadcast_select_fusion), channel_id=1, replica_groups=mesh['row'=8,'col'=4] {'row','col'}, dimensions={0}, use_global_device_ids=true | all-gather | bytes 135168 | tf_op jit(solution)/shard_map/all_gather | solution.py:54
  82.7 3.7 exponential_convert_fusion
  86.4 6.6 %select_reduce_fusion = (f32[]{:T(128)}, f32[1024,2048]{1,0:T(8,128)}) fusion(s32[2048]{0:T(1024)S(1)} %iota_add_fusion, s32[1024]{0:T(1024)S(1)} %iota_add_fusion.1, bf16[1024,512]{1,0:T(8,128)(2,1)S(1)} %exponential_convert_fusion.1, bf16[2048,512]{1,0:T(8,128)(2,1)S(1)} %exponential_convert_fusion), kind=kOutput, calls=%fused_computation.5 | convolution fusion | flops 2153775104 | bytes 11546628 | tf_op jit(solution)/shard_map/dot_general | solution.py:63
  93.0 41.1 %psum.35 = f32[]{:T(128)} all-reduce(f32[]{:T(128)} %get-tuple-element.38), channel_id=1, replica_groups=mesh['row'=8,'col'=4] {'row','col'}, use_global_device_ids=true, to_apply=%region_4.5 | all-reduce | flops 1 | bytes 8 | tf_op jit(solution)/shard_map/psum | solution.py:39
  134.2 9.3 %copy.22 = f32[1024,2048]{0,1:T(8,128)} copy(f32[1024,2048]{1,0:T(8,128)} %get-tuple-element.39) | data formatting | bytes 16777216 | tf_op jit(solution)/shard_map/dot_general | solution.py:63
  143.4 9.2 %copy.21 = f32[1024,2048]{0,1:T(8,128)} copy(f32[1024,2048]{1,0:T(8,128)} %param.13) | data formatting | bytes 16777216 | tf_op args[5]
  153.3 6.9 %divide_add_fusion = f32[1024,2048]{0,1:T(8,128)S(1)} fusion(f32[1024,2048]{0,1:T(8,128)} %copy.22, f32[1024,2048]{0,1:T(8,128)} %copy.21, f32[]{:T(128)S(6)} %div.41), kind=kLoop, calls=%fused_computation.4 | loop fusion | flops 8388608 | bytes 25165828 | tf_op jit(solution)/shard_map/add | solution.py:71
  160.2 3.4 copy-done.2
  164.8 3.0 dynamic-slice_select_fusion
  167.8 50.3 %all-reduce.6.cloned.1.call-done = f32[1024,256]{0,1:T(8,128)} async-done(((f32[1024,256]{0,1:T(8,128)}), f32[1024,256]{0,1:T(8,128)}) %all-reduce.6.cloned.1.call-update) | async-done | bytes 1048592 | tf_op jit(solution)/shard_map/psum | solution.py:16
  220.1 39.1 %all-reduce.1 = bf16[512]{0:T(512)(128)(2,1)S(1)} all-reduce(bf16[512]{0:T(512)(128)(2,1)S(1)} %dynamic-update-slice.15), channel_id=1, replica_groups=mesh['row'=8,'col'=4] {'row','col'}, use_global_device_ids=true, to_apply=%add.1 | all-reduce | flops 512 | bytes 2048
  261.1 12.8 %psum.39 = f32[256]{0:T(256)S(1)} all-reduce(f32[256]{0:T(256)S(1)} %dynamic-slice_select_fusion.3), channel_id=1, replica_groups=mesh['row'=8,'col'=4] {'row'}, use_global_device_ids=true, to_apply=%region_13.14 | all-reduce | flops 256 | bytes 2048 | tf_op jit(solution)/shard_map/psum | solution.py:16
  274.0 9.8 %all-reduce.8.cloned.1.call-done = (f32[256,256]{0,1:T(8,128)}, f32[256,2048]{0,1:T(8,128)}) async-done(((f32[256,256]{0,1:T(8,128)}, f32[256,2048]{0,1:T(8,128)}), (f32[256,256]{0,1:T(8,128)}, f32[256,2048]{0,1:T(8,128)})) %all-reduce.8.cloned.1.call-update) | async-done | bytes 2359312 | tf_op jit(solution)/shard_map/psum | solution.py:16
  285.8 11.7 %cholesky.49 = f32[128,128]{1,0:T(8,128)S(1)} custom-call(f32[128,128]{1,0:T(8,128)S(1)} %cholesky.115), custom_call_target="Cholesky" | custom-call | tf_op jit(solution)/shard_map/jit(cholesky)/cholesky | solution.py:91
  297.6 9.8 %custom-call.14 = f32[1,128,128]{1,2,0:T(8,128)S(1)} custom-call(f32[1,128,128]{2,1,0:T(8,128)S(1)} %get-tuple-element.37), custom_call_target="InvertDiagBlocksLowerTriangular" | custom-call | tf_op jit(solution)/shard_map/jit(cholesky)/cholesky | solution.py:91
  307.9 11.7 %cholesky.103 = f32[128,128]{1,0:T(8,128)S(1)} custom-call(f32[128,128]{1,0:T(8,128)S(1)} %convolution_subtract_fusion.2), custom_call_target="Cholesky" | custom-call | tf_op jit(solution)/shard_map/jit(cholesky)/cholesky | solution.py:91
  322.7 4.1 %while.1 = (s32[]{:T(128)}, f32[256,256]{0,1:T(8,128)S(1)}, s32[2,2]{1,0:T(2,128)S(1)}, f32[2,128,128]{2,1,0:T(8,128)S(1)}, s32[]{:T(128)}) while((s32[]{:T(128)}, f32[256,256]{0,1:T(8,128)S(1)}, s32[2,2]{1,0:T(2,128)S(1)}, f32[2,128,128]{2,1,0:T(8,128)S(1)}, s32[]{:T(128)}) %tuple.31), condition=%wide.while_cond, body=%wide.while_body.sunk | while | flops 2 | bytes 393321 | solution.py:93
  326.8 19.9 %custom-call.15 = f32[2,128,128]{1,2,0:T(8,128)S(1)} custom-call(f32[2,128,128]{2,1,0:T(8,128)S(1)} %get-tuple-element.9), custom_call_target="InvertDiagBlocksLowerTriangular" | custom-call | tf_op jit(solution)/shard_map/triangular_solve | solution.py:93
  347.6 3.5 fusion.9
  351.1 3.0 fusion.10
  355.6 11.2 %convolution_subtract_fusion = f32[1024,2048]{0,1:T(8,128)} fusion(f32[1024,2048]{0,1:T(8,128)} %copy-done.2, f32[1024,256]{1,0:T(8,128)S(1)} %fusion.10, f32[256,2048]{1,0:T(8,128)S(1)} %fusion.9), kind=kOutput, calls=%fused_computation.6 | convolution fusion | flops 6444548096 | bytes 19922944 | tf_op jit(solution)/shard_map/dot_general | solution.py:99
  369.9 2.5 select_dynamic-update-slice_fusion.1
  372.4 3.3 select_dynamic-update-slice_fusion
  377.4 9.1 %copy.31 = f32[1024,2048]{1,0:T(8,128)} copy(f32[1024,2048]{0,1:T(8,128)} %select_dynamic-update-slice_fusion.2) | data formatting | bytes 16777216
  (81 shorter events, 29.9 us)
Async XLA Ops:
  7.2 3.4 copy-start
  7.2 75.5 %copy-start.7 = (f32[128]{0:T(128)S(1)}, f32[128]{0:T(128)}, u32[]{:S(2)}) copy-start(f32[128]{0:T(128)} %param.12) | copy-start | bytes 1540
  7.2 210.9 %all-reduce.6.cloned.1.call-start = ((), (), s32[]{:S(2)}) async-start(), calls=%async_computation | async-start | bytes 2097152 | tf_op jit(solution)/shard_map/psum | solution.py:16
  160.2 3.4 copy-start.2
  164.7 96.3 %copy-start.8 = (f32[1024]{0:T(1024)S(1)}, f32[1024]{0:T(1024)}, u32[]{:S(2)}) copy-start(f32[1024]{0:T(1024)} %param.14) | copy-start | bytes 12292
  164.7 119.0 %all-reduce.8.cloned.1.call-start = ((), (), s32[]{:S(2)}) async-start(), calls=%async_computation.1 | async-start | bytes 4718592 | tf_op jit(solution)/shard_map/psum | solution.py:16
  321.9 0.7 copy-start.4
  368.6 3.8 copy-start.3
  369.9 5.8 %copy-start.5 = (f32[256,256]{0,1:T(8,128)S(1)}, f32[256,256]{0,1:T(8,128)}, u32[]{:S(2)}) copy-start(f32[256,256]{0,1:T(8,128)} %copy-done.4) | copy-start | bytes 786436
  377.4 9.9 %copy-start.1 = (bf16[128,128]{1,0:T(8,128)(2,1)S(1)}, bf16[128,128]{1,0:T(8,128)(2,1)}, u32[]{:S(2)}) copy-start(bf16[128,128]{1,0:T(8,128)(2,1)} %param.8) | copy-start | bytes 98308
  386.7 0.6 copy-start.6
Sparse Core Ops, SparseCore 0:
  164.8 53.2 all-reduce.5
  221.8 61.8 all-reduce.7
where the time goes:
time: 397 us; the launch traced here: 394 us
  blocking collectives  158 us (40%)
  other arithmetic  81 us (20%)
  waiting for transfers between devices  60.1 us (15%)
  local copies, waits for them, and re-layouts  43.2 us (11%)
  matrix products  33.5 us (8%)
  between operations  17.7 us (4%)
    all_gather x1, blocking collectives, local(): lax.all_gather(samples, ('row', 'col'), axis=0, tiled=True)  65.4 us
    psum x2, waiting for transfers between devices, spread(): return lax.psum(block, axis)  60.1 us
    psum x1, blocking collectives, diag_total(): return lax.psum(local_diag(gram_tile, row_base, col_base), ('row', 'col'))  41.1 us
    unnamed x1, blocking collectives  39.1 us
    another operation x6, other arithmetic, local(): factor = jnp.linalg.cholesky(got_block)  34 us
    unnamed x23, local copies, waits for them, and re-layouts  23.4 us
    another operation x3, other arithmetic, local(): lax.linalg.triangular_solve(factor, identity, left_side=True, lower=True)  19.9 us
    psum x1, blocking collectives, spread(): return lax.psum(block, axis)  12.8 us
  transfers between devices with their start and end apart: 2, of which 2 were waited for; matrix products, arithmetic and copies ran while one was open for 1% of the time, Pallas kernels for 0%

commit v1 on v0

v1 whole, which is shorter than its diff:
```python
import functools

import jax
import jax.numpy as jnp
from jax import lax
from jax.experimental import pallas as pl
from jax.experimental.pallas import tpu as pltpu
from jax.sharding import PartitionSpec as P

PB = 256
RATE = 0.5
EPSILON = 1e-05
SUPER = 64
SUB = 8
LANES = 128
ROWS_STEP = 256
F32 = jnp.float32
BF16 = jnp.bfloat16
HIGHEST = lax.Precision.HIGHEST
NN = (((1,), (0,)), ((), ()))
NT = (((1,), (1,)), ((), ()))
TN = (((0,), (0,)), ((), ()))
MESH = pl.DeviceIdType.MESH


def dot(a, b, dims, precision=None):
    return lax.dot_general(a, b, dims, precision=precision, preferred_element_type=F32)


def split_two(x):
    high = x.astype(BF16)
    return high, (x - high.astype(F32)).astype(BF16)


def dot_split(a, b, dims):
    a_high, a_low = a
    b_high, b_low = b
    return dot(a_high, b_high, dims) + (dot(a_high, b_low, dims) + dot(a_low, b_high, dims))


def prep_kernel(
    info, picks_ref, pool_ref, targets_ref, cols_ref, rows_ref, diag_ref, mean_ref, points_ref,
    xs_out, cols_out, rows_out, diag_out, points_out,
):
    in_row = info[2] == 1
    in_col = info[3] == 1
    pool_count = pool_ref.shape[0]
    batch = picks_ref.shape[1]
    ids = lax.broadcasted_iota(jnp.int32, (pool_count, batch), 0)
    chosen_t = jnp.where(ids == picks_ref[...], 1.0, 0.0).astype(BF16)
    eye = jnp.where(
        lax.broadcasted_iota(jnp.int32, (pool_count, pool_count), 0)
        == lax.broadcasted_iota(jnp.int32, (pool_count, pool_count), 1),
        1.0,
        0.0,
    ).astype(BF16)
    chosen = dot(chosen_t, eye, TN)
    values = jnp.sum(chosen * targets_ref[...].astype(F32), axis=1, keepdims=True)
    samples = dot(chosen_t, pool_ref[...], TN)
    width = samples.shape[1]
    xs_out[:, :width] = samples.astype(BF16)
    xs_out[:, width:] = jnp.broadcast_to(values, (batch, LANES)).astype(BF16)
    zero = jnp.float32(0.0)
    cols_out[...] = jnp.where(in_col, cols_ref[...], zero).astype(BF16)
    rows_out[...] = jnp.where(in_row, rows_ref[...], zero).astype(BF16)
    points_out[...] = points_ref[...]
    both = jnp.logical_and(in_row, in_col)
    diag_out[:PB, :] = jnp.where(both, diag_ref[...], zero)
    diag_out[PB:, :] = jnp.where(
        both, jnp.broadcast_to(mean_ref[...], (diag_out.shape[0] - PB, PB)), zero
    )


def feature_block(points, weights, samples_twice, samples_sq):
    scaled = points * weights
    point_sq = jnp.sum(points * scaled, axis=1, keepdims=True)
    high, low = split_two(scaled)
    cross_term = dot(jnp.concatenate([high, low], axis=1), samples_twice, NT)
    return jnp.exp(cross_term - 0.5 * (point_sq + samples_sq)).astype(BF16)


def eliminate_super(x_ref, base):
    sub_ids = lax.broadcasted_iota(jnp.int32, (SUB, LANES), 0)
    groups = SUPER // SUB
    size = x_ref.shape[0]
    for step in range(groups):
        col0 = base + step * SUB
        lane_tiles = [t for t in range(size // LANES) if (t + 1) * LANES > col0]
        lane_tiles += [size // LANES + t for t in range(size // LANES) if t * LANES < col0 + SUB]
        rows = {
            g: x_ref[base + g * SUB : base + (g + 1) * SUB, col0 : col0 + SUB]
            for g in range(step, groups)
        }
        column = {
            g: [jnp.broadcast_to(rows[g][:, k : k + 1], (SUB, LANES)) for k in range(SUB)]
            for g in rows
        }
        square = {
            (m, k): jnp.broadcast_to(column[step][k][m : m + 1, :], (SUB, LANES))
            for k in range(SUB)
            for m in range(k + 1)
        }
        scale = []
        below = {}
        for k in range(SUB):
            scale.append(lax.rsqrt(square[k, k]))
            for j in range(k + 1, SUB):
                below[j, k] = square[k, j] * scale[k]
            for m in range(k + 1, SUB):
                for j in range(m, SUB):
                    square[m, j] = square[m, j] - below[m, k] * below[j, k]
        factor_cols = {}
        for g in rows:
            for k in range(SUB):
                value = column[g][k]
                for m in range(k):
                    value = value - factor_cols[g, m] * below[k, m]
                factor_cols[g, k] = value * scale[k]
        for t in lane_tiles:
            lanes = slice(t * LANES, (t + 1) * LANES)
            tiles = {
                g: x_ref[base + g * SUB : base + (g + 1) * SUB, lanes] for g in range(step, groups)
            }
            for k in range(SUB):
                pivot_row = jnp.broadcast_to(tiles[step][k : k + 1, :], (SUB, LANES)) * scale[k]
                mine = tiles[step] - jnp.where(sub_ids > k, factor_cols[step, k], 0.0) * pivot_row
                tiles[step] = jnp.where(sub_ids == k, pivot_row, mine)
                for g in range(step + 1, groups):
                    tiles[g] = tiles[g] - factor_cols[g, k] * pivot_row
            for g in tiles:
                x_ref[base + g * SUB : base + (g + 1) * SUB, lanes] = tiles[g]
    after = base + SUPER
    if after < size:
        done = x_ref[base:after, :]
        x_ref[after:, :] = x_ref[after:, :] - dot(done[:, after:size], done, TN, HIGHEST)


def move_kernel(
    n_rows, n_cols,
    points_ref, xs_ref, cols_ref, rows_ref, diag_ref, inducing_ref, weights_ref,
    feat_r_out, feat_c_out, feat_p_out, cols_out, rows_out, x_out, mean_out, stats_out, y_out,
    all_x, diag_got, diag_sum, diag_col, diag_all, cols_got, cols_sum, rows_got, rows_sum, twice,
    send_sem, recv_sem,
):
    my_row = lax.axis_index("row")
    my_col = lax.axis_index("col")
    n_of = {"row": n_rows, "col": n_cols}
    me_of = {"row": my_row, "col": my_col}
    slot = [0]

    def peer(axis, distance):
        return lax.rem(me_of[axis] + distance, n_of[axis])

    def peer_id(axis, distance):
        if axis == "row":
            return (peer(axis, distance), my_col)
        return (my_row, peer(axis, distance))

    def send_all(axis, source, target):
        copies = []
        for distance in range(1, n_of[axis]):
            copy = pltpu.make_async_remote_copy(
                src_ref=source(distance),
                dst_ref=target(distance),
                send_sem=send_sem.at[slot[0]],
                recv_sem=recv_sem.at[slot[0]],
                device_id=peer_id(axis, distance),
                device_id_type=MESH,
            )
            slot[0] += 1
            copy.start()
            copies.append(copy)
        return copies

    def arrive(copies):
        for copy in copies:
            copy.wait_recv()

    started = []

    barrier = pltpu.get_barrier_semaphore()
    for axis in ("row", "col"):
        for distance in range(1, n_of[axis]):
            pl.semaphore_signal(
                barrier, inc=1, device_id=peer_id(axis, distance), device_id_type=MESH
            )
    pl.semaphore_wait(barrier, n_rows + n_cols - 2)

    batch = xs_ref.shape[0]
    all_x[my_col, my_row] = xs_ref[...]
    xs_first = send_all("row", lambda d: xs_ref, lambda d: all_x.at[my_col, my_row])

    def slices(count, ref, axis):
        return lambda d: ref.at[pl.ds(peer(axis, d) * count, count)]

    diag_count = diag_sum.shape[0]
    diag_first = send_all(
        "row", slices(diag_count, diag_ref, "row"), lambda d: diag_got.at[d - 1]
    )
    arrive(xs_first)
    xs_second = send_all("col", lambda d: all_x.at[my_col], lambda d: all_x.at[my_col])

    def combine(ref, got, axis, count):
        total = ref[pl.ds(me_of[axis] * count, count), :]
        for distance in range(1, n_of[axis]):
            total = total + got[distance - 1]
        return total

    arrive(diag_first)
    diag_sum[...] = combine(diag_ref, diag_got, "row", diag_count)
    diag_second = send_all("col", lambda d: diag_sum, lambda d: diag_col.at[d - 1])
    rows_count = rows_sum.shape[0]
    rows_first = send_all(
        "row", slices(rows_count, rows_ref, "row"), lambda d: rows_got.at[d - 1]
    )
    cols_count = cols_sum.shape[0]
    arrive(diag_second)
    total = diag_sum[...]
    for distance in range(1, n_cols):
        total = total + diag_col[distance - 1]
    diag_mine = pl.ds(my_row * diag_count, diag_count)
    diag_all[diag_mine, :] = total
    diag_third = send_all("row", lambda d: diag_all.at[diag_mine], lambda d: diag_all.at[diag_mine])
    arrive(xs_second)
    cols_first = send_all(
        "col", slices(cols_count, cols_ref, "col"), lambda d: cols_got.at[d - 1]
    )

    width = inducing_ref.shape[1]
    n_batch = n_rows * n_cols * batch
    gathered = all_x[...].reshape(n_batch, all_x.shape[3])
    samples = gathered[:, :width]
    twice[:, :width] = samples
    twice[:, width:] = samples
    values_t = jnp.transpose(gathered[:, width:].astype(F32))[:SUB, :]
    y_out[...] = values_t.astype(BF16)
    power = jnp.sum(values_t[:1, :] * values_t[:1, :], keepdims=True)
    weights = weights_ref[...]
    samples_f = samples.astype(F32)
    samples_sq = dot(jnp.broadcast_to(weights, (SUB, width)), samples_f * samples_f, NT, HIGHEST)[:1, :]

    tile_rows = feat_r_out.shape[0]
    tile_cols = feat_c_out.shape[0]
    points_count = inducing_ref.shape[0]

    def features_of(points):
        return feature_block(points, weights, twice[...], samples_sq)

    def trace_step(index, total):
        start = pl.multiple_of(index * PB, PB)
        block = features_of(inducing_ref[pl.ds(start, PB), :])

        @pl.when(start // tile_rows == my_row)
        def _():
            feat_r_out[pl.ds(pl.multiple_of(lax.rem(start, tile_rows), PB), PB), :] = block

        @pl.when(start // tile_cols == my_col)
        def _():
            feat_c_out[pl.ds(pl.multiple_of(lax.rem(start, tile_cols), PB), PB), :] = block

        wide = block.astype(F32)
        return total + jnp.sum((wide * wide).reshape(PB // SUB, SUB, n_batch), axis=0)

    partial = lax.fori_loop(
        0, points_count // PB, trace_step, jnp.zeros((SUB, n_batch), F32)
    )
    trace_scale = jnp.sum(partial, keepdims=True) / points_count
    gram_scale = RATE / trace_scale
    mean_scale = RATE * lax.rsqrt(trace_scale * (power / n_batch + EPSILON))
    stats_out[0:1, :] = jnp.broadcast_to(gram_scale, (1, LANES))
    stats_out[1:2, :] = jnp.broadcast_to(mean_scale, (1, LANES))
    stats_out[2:, :] = jnp.zeros((SUB - 2, LANES), F32)

    arrive(rows_first)
    rows_sum[...] = combine(rows_ref, rows_got, "row", rows_count)
    rows_mine = pl.ds(my_row * rows_count, rows_count)
    rows_out[rows_mine, :] = rows_sum[...]
    rows_second = send_all("row", lambda d: rows_sum, lambda d: rows_out.at[rows_mine])

    feat_p = features_of(points_ref[...])
    feat_p_out[...] = feat_p
    gram_p = dot(feat_p, feat_p, NT)
    arrive(diag_third)
    mean_out[...] = diag_all[PB : PB + SUB, :]
    x_out[:, :PB] = (1.0 - RATE) * diag_all[:PB, :] + gram_scale * gram_p
    x_out[:, PB:] = jnp.where(
        lax.broadcasted_iota(jnp.int32, (PB, PB), 0) == lax.broadcasted_iota(jnp.int32, (PB, PB), 1),
        1.0,
        0.0,
    )
    for base in range(0, PB, SUPER):
        eliminate_super(x_out, base)
        if base == 0:
            arrive(cols_first)
            cols_sum[...] = combine(cols_ref, cols_got, "col", cols_count)
            cols_mine = pl.ds(my_col * cols_count, cols_count)
            cols_out[cols_mine, :] = cols_sum[...]
            cols_second = send_all("col", lambda d: cols_sum, lambda d: cols_out.at[cols_mine])
    arrive(rows_second)
    arrive(cols_second)
    for copies in (
        xs_first, xs_second, diag_first, diag_second, diag_third,
        rows_first, rows_second, cols_first, cols_second,
    ):
        for copy in copies:
            copy.wait_send()


def tile_kernel(
    info,
    prec_ref, feat_r_ref, feat_c_ref, feat_p_ref, cols_ref, rows_ref, x_ref, mean_p_ref,
    stats_ref, y_ref, mean_ref,
    out_ref, mean_out,
    solved, solved_high, solved_low, inverse_high, inverse_low, head,
):
    step = pl.program_id(0)
    in_row = info[2] == 1
    in_col = info[3] == 1
    keep = 1.0 - RATE
    gram_scale = stats_ref[0:1, 0:1]
    mean_scale = stats_ref[1:2, 0:1]

    @pl.when(step == 0)
    def _():
        inverse = x_ref[:, PB:]
        high, low = split_two(inverse)
        inverse_high[...] = high
        inverse_low[...] = low
        joined = keep * rows_ref[...].astype(F32) + gram_scale * dot(feat_p_ref[...], feat_c_ref[...], NT)
        result = dot_split((high, low), split_two(joined), NN)
        solved[...] = result
        solved_high[...], solved_low[...] = split_two(result)
        fit = dot(y_ref[...], feat_p_ref[...], NT)
        head[...] = dot(keep * mean_p_ref[...] + mean_scale * fit, inverse, NT, HIGHEST)

    feat_r = feat_r_ref[...]
    piece = keep * cols_ref[...].astype(F32) + gram_scale * dot(feat_r, feat_p_ref[...], NT)
    wide = dot_split(split_two(piece), (inverse_high[...], inverse_low[...]), NT)
    wide_high, wide_low = split_two(wide)
    tile = keep * prec_ref[...] + gram_scale * dot(feat_r, feat_c_ref[...], NT)
    out_ref[...] = tile - dot_split(
        (wide_high, wide_low), (solved_high[...], solved_low[...]), NN
    )
    fit = dot(y_ref[...], feat_r, NT)
    mean_next = (
        keep * mean_ref[...] + mean_scale * fit[:1, :] - dot(head[...], wide, NT, HIGHEST)[:1, :]
    )
    mean_out[...] = mean_next
    col0 = pl.multiple_of(info[1] * PB, PB)

    @pl.when(in_col)
    def _():
        out_ref[:, pl.ds(col0, PB)] = wide

    here = jnp.logical_and(in_row, step == info[0])

    @pl.when(here)
    def _():
        out_ref[...] = solved[...]
        mean_out[...] = head[:1, :]

    @pl.when(jnp.logical_and(here, in_col))
    def _():
        factor = jnp.transpose(x_ref[:, :PB])
        lower = lax.broadcasted_iota(jnp.int32, (PB, PB), 0) >= lax.broadcasted_iota(
            jnp.int32, (PB, PB), 1
        )
        out_ref[:, pl.ds(col0, PB)] = jnp.where(lower, factor, 0.0)


def whole(memory=pltpu.VMEM):
    return pl.BlockSpec(memory_space=memory)


def local(pool, targets, picks, inducing, inv_sq_lengths, prec_old, mean_old, panel):
    n_rows = lax.axis_size("row")
    n_cols = lax.axis_size("col")
    my_row = lax.axis_index("row")
    my_col = lax.axis_index("col")
    tile_rows, tile_cols = prec_old.shape
    batch = picks.shape[0]
    n_batch = batch * n_rows * n_cols
    width = pool.shape[1]
    row_blocks = tile_rows // PB
    col_blocks = tile_cols // PB
    index = panel[0]
    info = jnp.stack(
        [
            lax.rem(index, row_blocks),
            lax.rem(index, col_blocks),
            (index // row_blocks == my_row).astype(jnp.int32),
            (index // col_blocks == my_col).astype(jnp.int32),
            index,
        ]
    )
    mean_row = mean_old.reshape(1, tile_rows)
    shape = jax.ShapeDtypeStruct
    diag_count = -(-(PB + SUB) // (n_rows * SUB)) * SUB
    diag_rows = diag_count * n_rows
    full = lambda *dims: pl.BlockSpec(dims, lambda i, info: (0,) * len(dims))
    xs, cols, rows, diag, points = pl.pallas_call(
        prep_kernel,
        grid_spec=pltpu.PrefetchScalarGridSpec(
            num_scalar_prefetch=1,
            grid=(1,),
            in_specs=[
                full(1, batch),
                full(*pool.shape),
                full(1, pool.shape[0]),
                pl.BlockSpec((tile_rows, PB), lambda i, info: (0, info[1])),
                pl.BlockSpec((PB, tile_cols), lambda i, info: (info[0], 0)),
                pl.BlockSpec((PB, PB), lambda i, info: (info[0], info[1])),
                pl.BlockSpec((1, PB), lambda i, info: (0, info[0])),
                pl.BlockSpec((PB, width), lambda i, info: (info[4], 0)),
            ],
            out_specs=[
                full(batch, width + LANES),
                full(tile_rows, PB),
                full(PB, tile_cols),
                full(diag_rows, PB),
                full(PB, width),
            ],
        ),
        out_shape=[
            shape((batch, width + LANES), BF16),
            shape((tile_rows, PB), BF16),
            shape((PB, tile_cols), BF16),
            shape((diag_rows, PB), F32),
            shape((PB, width), F32),
        ],
        compiler_params=pltpu.CompilerParams(vmem_limit_bytes=40 << 20),
        name="prep",
    )(
        info, picks.reshape(1, batch), pool, targets.reshape(1, -1),
        prec_old, prec_old, prec_old, mean_row, inducing,
    )
    sems = 5 * (n_rows - 1) + 4 * (n_cols - 1)
    cols_count = tile_rows // n_cols
    rows_count = PB // n_rows
    moved = pl.pallas_call(
        functools.partial(move_kernel, n_rows, n_cols),
        in_specs=[whole()] * 7,
        out_specs=[whole()] * 9,
        out_shape=[
            shape((tile_rows, n_batch), BF16),
            shape((tile_cols, n_batch), BF16),
            shape((PB, n_batch), BF16),
            shape((tile_rows, PB), BF16),
            shape((PB, tile_cols), BF16),
            shape((PB, 2 * PB), F32),
            shape((SUB, PB), F32),
            shape((SUB, LANES), F32),
            shape((SUB, n_batch), BF16),
        ],
        scratch_shapes=[
            pltpu.VMEM((n_cols, n_rows, batch, width + LANES), BF16),
            pltpu.VMEM((n_rows - 1, diag_count, PB), F32),
            pltpu.VMEM((diag_count, PB), F32),
            pltpu.VMEM((n_cols - 1, diag_count, PB), F32),
            pltpu.VMEM((diag_rows, PB), F32),
            pltpu.VMEM((n_cols - 1, cols_count, PB), BF16),
            pltpu.VMEM((cols_count, PB), BF16),
            pltpu.VMEM((n_rows - 1, rows_count, tile_cols), BF16),
            pltpu.VMEM((rows_count, tile_cols), BF16),
            pltpu.VMEM((n_batch, 2 * width), BF16),
            pltpu.SemaphoreType.DMA((sems,)),
            pltpu.SemaphoreType.DMA((sems,)),
        ],
        compiler_params=pltpu.CompilerParams(
            collective_id=0, has_side_effects=True, vmem_limit_bytes=56 << 20
        ),
        name="move",
    )(points, xs, cols, rows, diag, inducing, inv_sq_lengths.reshape(1, width))
    feat_r, feat_c, feat_p, got_cols, got_rows, x, mean_p, stats, y = moved
    step_rows = PB
    updated, mean_next = pl.pallas_call(
        tile_kernel,
        grid_spec=pltpu.PrefetchScalarGridSpec(
            num_scalar_prefetch=1,
            grid=(tile_rows // step_rows,),
            in_specs=[
                pl.BlockSpec((step_rows, tile_cols), lambda i, info: (i, 0)),
                pl.BlockSpec((step_rows, n_batch), lambda i, info: (i, 0)),
                full(tile_cols, n_batch),
                full(PB, n_batch),
                pl.BlockSpec((step_rows, PB), lambda i, info: (i, 0)),
                full(PB, tile_cols),
                full(PB, 2 * PB),
                full(SUB, PB),
                full(SUB, LANES),
                full(SUB, n_batch),
                pl.BlockSpec((1, step_rows), lambda i, info: (0, i)),
            ],
            out_specs=[
                pl.BlockSpec((step_rows, tile_cols), lambda i, info: (i, 0)),
                pl.BlockSpec((1, step_rows), lambda i, info: (0, i)),
            ],
            scratch_shapes=[
                pltpu.VMEM((PB, tile_cols), F32),
                pltpu.VMEM((PB, tile_cols), BF16),
                pltpu.VMEM((PB, tile_cols), BF16),
                pltpu.VMEM((PB, PB), BF16),
                pltpu.VMEM((PB, PB), BF16),
                pltpu.VMEM((SUB, PB), F32),
            ],
        ),
        out_shape=[shape((tile_rows, tile_cols), F32), shape((1, tile_rows), F32)],
        compiler_params=pltpu.CompilerParams(vmem_limit_bytes=56 << 20),
        name="tile",
    )(
        info, prec_old, feat_r, feat_c, feat_p, got_cols, got_rows, x, mean_p, stats, y, mean_row,
    )
    return updated, mean_next.reshape(tile_rows)


def solution(mesh):
    in_specs = (
        P(("row", "col"), None),
        P(("row", "col")),
        P(("row", "col")),
        P(),
        P(),
        P("row", "col"),
        P("row"),
        P(),
    )
    out_specs = (P("row", "col"), P("row"))
    return jax.shard_map(local, mesh=mesh, in_specs=in_specs, out_specs=out_specs, check_vma=False)
```

time: 397 us -> 80.8 us (0.20)
  the two profiles are of different devices: /device:TPU:1 before, /device:TPU:0 now
where the time goes in v1:
time: 80.8 us; the launch traced here: 80.4 us
  Pallas kernels  70.2 us (87%)
  local copies, waits for them, and re-layouts  8.81 us (11%)
  between operations  1.36 us (2%)
    pallas_call x1, Pallas kernels, local(): pl.pallas_call(functools.partial(move_kernel, n_rows, n_cols), in_specs=[...  51.2 us
    pallas_call x1, Pallas kernels, local(): pl.pallas_call(tile_kernel, grid_spec=pltpu.PrefetchScalarGridSpec(num_sc...  16.2 us
    unnamed x22, local copies, waits for them, and re-layouts  8.72 us
    pallas_call x1, Pallas kernels, local(): pl.pallas_call(prep_kernel, grid_spec=pltpu.PrefetchScalarGridSpec(num_sc...  2.8 us

profile of v1, /device:TPU:0, one launch (start us, length us, event | category | flops | bytes accessed | tf_op | source)
XLA Modules:
  0.0 80.4 jit_solution(4545633992425968973)
XLA Ops:
  1.3 0.1 stack.27.info
  1.4 0.0 copy-start.8
  1.4 0.0 copy-start
  1.4 2.2 %copy-done = f32[8192,128]{1,0:T(8,128)S(1)} copy-done((f32[8192,128]{1,0:T(8,128)S(1)}, f32[8192,128]{1,0:T(8,128)}, u32[]{:S(2)}) %copy-start) | copy-done | bytes 4194328
  3.6 0.0 copy-start.5
  3.6 0.8 copy-done.5
  4.4 0.0 copy-start.6
  4.4 0.7 copy-done.6
  5.0 0.0 copy-start.9
  5.0 0.7 copy-done.9
  5.7 0.0 copy-start.10
  5.7 0.7 copy-done.10
  6.4 2.8 %prep.1 = (bf16[16,256]{1,0:T(8,128)(2,1)S(1)}, bf16[1024,256]{1,0:T(8,128)(2,1)S(1)}, bf16[256,2048]{1,0:T(8,128)(2,1)S(1)}, f32[320,256]{1,0:T(8,128)S(1)}, f32[256,128]{1,0:T(8,128)S(1)}) custom-call(s32[5]{0:T(128)S(1)} %stack.27.info, s32[1,16]{1,0:T(1,128)S(1)} %bitcast.16, bf16[128,128]{1,0:T(8,128)(2,1)S(1)} %copy-done.5, ...), custom_call_target="tpu_custom_call" | custom-call | tf_op jit(solution)/shard_map/prep/pallas_call | solution.py:401
  9.2 0.0 copy-done.8
  9.2 0.0 copy-start.1
  9.2 1.0 %copy-done.1 = bf16[256,2048]{1,0:T(8,128)(2,1)} copy-done((bf16[256,2048]{1,0:T(8,128)(2,1)}, bf16[256,2048]{1,0:T(8,128)(2,1)S(1)}, u32[]{:S(2)}) %copy-start.1) | copy-done | bytes 1048600
  10.1 0.0 copy-start.2
  10.1 0.8 %copy-done.2 = bf16[1024,256]{1,0:T(8,128)(2,1)} copy-done((bf16[1024,256]{1,0:T(8,128)(2,1)}, bf16[1024,256]{1,0:T(8,128)(2,1)S(1)}, u32[]{:S(2)}) %copy-start.2) | copy-done | bytes 524312
  11.0 0.0 copy-start.3
  11.0 0.7 copy-done.3
  11.7 0.6 copy-done.4
  12.4 0.6 copy-done.7
  13.0 51.2 %move.1 = (bf16[1024,512]{1,0:T(8,128)(2,1)}, bf16[2048,512]{1,0:T(8,128)(2,1)}, bf16[256,512]{1,0:T(8,128)(2,1)}, bf16[1024,256]{1,0:T(8,128)(2,1)}, bf16[256,2...) custom-call(f32[256,128]{1,0:T(8,128)} %copy-done.4, ...), custom_call_target="tpu_custom_call" | custom-call | tf_op jit(solution)/shard_map/move/pallas_call | solution.py:440
  64.2 16.2 %tile.1 = (f32[1024,2048]{1,0:T(8,128)}, f32[1,1024]{1,0:T(1,128)}) custom-call(s32[5]{0:T(128)} %copy-done.8, f32[1024,2048]{1,0:T(8,128)} %prec_ref.1, bf16[1024,512]{1,0:T(8,128)(2,1)} %get-tuple-element.23.feat_r_ref, bf16[2048,512]{1,0:T(8,128)(2,1)} %get-tuple-element.24.feat_c_ref, bf16[256,512]{1,0:T(8,128)(2,1)} %get-tuple-element.25.feat_p_ref, ...), custom_call_target="tpu_custom_call" | custom-call | tf_op jit(solution)/shard_map/tile/pallas_call | solution.py:476
  (2 shorter events, 0.0 us)
Async XLA Ops:
  1.4 7.8 %copy-start.8 = (s32[5]{0:T(128)}, s32[5]{0:T(128)S(1)}, u32[]{:S(2)}) copy-start(s32[5]{0:T(128)S(1)} %stack.27.info) | copy-start | bytes 64
  1.4 2.2 %copy-start = (f32[8192,128]{1,0:T(8,128)S(1)}, f32[8192,128]{1,0:T(8,128)}, u32[]{:S(2)}) copy-start(f32[8192,128]{1,0:T(8,128)} %inducing_ref.1) | copy-start | bytes 12582916
  3.6 0.8 copy-start.5
  4.4 0.7 copy-start.6
  5.0 0.7 copy-start.9
  5.7 0.7 copy-start.10
  9.2 1.0 %copy-start.1 = (bf16[256,2048]{1,0:T(8,128)(2,1)}, bf16[256,2048]{1,0:T(8,128)(2,1)S(1)}, u32[]{:S(2)}) copy-start(bf16[256,2048]{1,0:T(8,128)(2,1)S(1)} %get-tuple-element.21.rows_ref) | copy-start | bytes 3145732
  10.1 0.8 %copy-start.2 = (bf16[1024,256]{1,0:T(8,128)(2,1)}, bf16[1024,256]{1,0:T(8,128)(2,1)S(1)}, u32[]{:S(2)}) copy-start(bf16[1024,256]{1,0:T(8,128)(2,1)S(1)} %get-tuple-element.20.cols_ref) | copy-start | bytes 1572868
  11.0 0.7 copy-start.3
  11.7 0.6 copy-start.4
  12.4 0.6 copy-start.7

commit v2 on v1

--- a/solution.py
+++ b/solution.py
@@ -13,7 +13,7 @@
 SUPER = 64
 SUB = 8
 LANES = 128
-ROWS_STEP = 256
+VMEM = 62 << 20
 F32 = jnp.float32
 BF16 = jnp.bfloat16
 HIGHEST = lax.Precision.HIGHEST
@@ -76,7 +76,7 @@
     point_sq = jnp.sum(points * scaled, axis=1, keepdims=True)
     high, low = split_two(scaled)
     cross_term = dot(jnp.concatenate([high, low], axis=1), samples_twice, NT)
-    return jnp.exp(cross_term - 0.5 * (point_sq + samples_sq)).astype(BF16)
+    return jnp.exp(cross_term - 0.5 * (point_sq + samples_sq))
 
 
 def eliminate_super(x_ref, base):
@@ -139,8 +139,9 @@
     n_rows, n_cols,
     points_ref, xs_ref, cols_ref, rows_ref, diag_ref, inducing_ref, weights_ref,
     feat_r_out, feat_c_out, feat_p_out, cols_out, rows_out, x_out, mean_out, stats_out, y_out,
+    points_v, feat_r, feat_c,
     all_x, diag_got, diag_sum, diag_col, diag_all, cols_got, cols_sum, rows_got, rows_sum, twice,
-    send_sem, recv_sem,
+    send_sem, recv_sem, local_sem,
 ):
     my_row = lax.axis_index("row")
     my_col = lax.axis_index("col")
@@ -176,7 +177,8 @@
         for copy in copies:
             copy.wait_recv()
 
-    started = []
+    load_points = pltpu.make_async_copy(inducing_ref, points_v, local_sem.at[0])
+    load_points.start()
 
     barrier = pltpu.get_barrier_semaphore()
     for axis in ("row", "col"):
@@ -193,38 +195,33 @@
     def slices(count, ref, axis):
         return lambda d: ref.at[pl.ds(peer(axis, d) * count, count)]
 
-    diag_count = diag_sum.shape[0]
-    diag_first = send_all(
-        "row", slices(diag_count, diag_ref, "row"), lambda d: diag_got.at[d - 1]
-    )
-    arrive(xs_first)
-    xs_second = send_all("col", lambda d: all_x.at[my_col], lambda d: all_x.at[my_col])
-
     def combine(ref, got, axis, count):
         total = ref[pl.ds(me_of[axis] * count, count), :]
         for distance in range(1, n_of[axis]):
             total = total + got[distance - 1]
         return total
 
+    diag_count = diag_sum.shape[0]
+    rows_count = rows_sum.shape[0]
+    cols_count = cols_sum.shape[0]
+    diag_mine = pl.ds(my_row * diag_count, diag_count)
+    rows_mine = pl.ds(my_row * rows_count, rows_count)
+    cols_mine = pl.ds(my_col * cols_count, cols_count)
+    diag_first = send_all(
+        "row", slices(diag_count, diag_ref, "row"), lambda d: diag_got.at[d - 1]
+    )
+    arrive(xs_first)
+    xs_second = send_all("col", lambda d: all_x.at[my_col], lambda d: all_x.at[my_col])
+    cols_first = send_all(
+        "col", slices(cols_count, cols_ref, "col"), lambda d: cols_got.at[d - 1]
+    )
     arrive(diag_first)
     diag_sum[...] = combine(diag_ref, diag_got, "row", diag_count)
     diag_second = send_all("col", lambda d: diag_sum, lambda d: diag_col.at[d - 1])
-    rows_count = rows_sum.shape[0]
     rows_first = send_all(
         "row", slices(rows_count, rows_ref, "row"), lambda d: rows_got.at[d - 1]
     )
-    cols_count = cols_sum.shape[0]
-    arrive(diag_second)
-    total = diag_sum[...]
-    for distance in range(1, n_cols):
-        total = total + diag_col[distance - 1]
-    diag_mine = pl.ds(my_row * diag_count, diag_count)
-    diag_all[diag_mine, :] = total
-    diag_third = send_all("row", lambda d: diag_all.at[diag_mine], lambda d: diag_all.at[diag_mine])
     arrive(xs_second)
-    cols_first = send_all(
-        "col", slices(cols_count, cols_ref, "col"), lambda d: cols_got.at[d - 1]
-    )
 
     width = inducing_ref.shape[1]
     n_batch = n_rows * n_cols * batch
@@ -239,31 +236,55 @@
     samples_f = samples.astype(F32)
     samples_sq = dot(jnp.broadcast_to(weights, (SUB, width)), samples_f * samples_f, NT, HIGHEST)[:1, :]
 
-    tile_rows = feat_r_out.shape[0]
-    tile_cols = feat_c_out.shape[0]
+    tile_rows = feat_r.shape[0]
+    tile_cols = feat_c.shape[0]
     points_count = inducing_ref.shape[0]
 
     def features_of(points):
         return feature_block(points, weights, twice[...], samples_sq)
 
+    step_rows = min(2 * PB, tile_rows, tile_cols)
+
     def trace_step(index, total):
-        start = pl.multiple_of(index * PB, PB)
-        block = features_of(inducing_ref[pl.ds(start, PB), :])
+        start = pl.multiple_of(index * step_rows, step_rows)
+        exact = features_of(points_v[pl.ds(start, step_rows), :])
+        block = exact.astype(BF16)
 
         @pl.when(start // tile_rows == my_row)
         def _():
-            feat_r_out[pl.ds(pl.multiple_of(lax.rem(start, tile_rows), PB), PB), :] = block
+            feat_r[pl.ds(pl.multiple_of(lax.rem(start, tile_rows), step_rows), step_rows), :] = block
 
         @pl.when(start // tile_cols == my_col)
         def _():
-            feat_c_out[pl.ds(pl.multiple_of(lax.rem(start, tile_cols), PB), PB), :] = block
-
-        wide = block.astype(F32)
-        return total + jnp.sum((wide * wide).reshape(PB // SUB, SUB, n_batch), axis=0)
-
-    partial = lax.fori_loop(
-        0, points_count // PB, trace_step, jnp.zeros((SUB, n_batch), F32)
-    )
+            feat_c[pl.ds(pl.multiple_of(lax.rem(start, tile_cols), step_rows), step_rows), :] = block
+
+        return total + jnp.sum((exact * exact).reshape(step_rows // SUB, SUB, n_batch), axis=0)
+
+    load_points.wait()
+    partial = jnp.zeros((SUB, n_batch), F32)
+    quarter = points_count // step_rows // 4
+    for part in range(4):
+        partial = lax.fori_loop(part * quarter, (part + 1) * quarter, trace_step, partial)
+        if part == 1:
+            arrive(diag_second)
+            total = diag_sum[...]
+            for distance in range(1, n_cols):
+                total = total + diag_col[distance - 1]
+            diag_all[diag_mine, :] = total
+            diag_third = send_all(
+                "row", lambda d: diag_all.at[diag_mine], lambda d: diag_all.at[diag_mine]
+            )
+        if part == 2:
+            arrive(cols_first)
+            cols_sum[...] = combine(cols_ref, cols_got, "col", cols_count)
+            cols_out[cols_mine, :] = cols_sum[...]
+            cols_second = send_all("col", lambda d: cols_sum, lambda d: cols_out.at[cols_mine])
+    stores = [
+        pltpu.make_async_copy(feat_r, feat_r_out, local_sem.at[1]),
+        pltpu.make_async_copy(feat_c, feat_c_out, local_sem.at[2]),
+    ]
+    for store in stores:
+        store.start()
     trace_scale = jnp.sum(partial, keepdims=True) / points_count
     gram_scale = RATE / trace_scale
     mean_scale = RATE * lax.rsqrt(trace_scale * (power / n_batch + EPSILON))
@@ -273,11 +294,10 @@
 
     arrive(rows_first)
     rows_sum[...] = combine(rows_ref, rows_got, "row", rows_count)
-    rows_mine = pl.ds(my_row * rows_count, rows_count)
     rows_out[rows_mine, :] = rows_sum[...]
     rows_second = send_all("row", lambda d: rows_sum, lambda d: rows_out.at[rows_mine])
 
-    feat_p = features_of(points_ref[...])
+    feat_p = features_of(points_ref[...]).astype(BF16)
     feat_p_out[...] = feat_p
     gram_p = dot(feat_p, feat_p, NT)
     arrive(diag_third)
@@ -290,12 +310,6 @@
     )
     for base in range(0, PB, SUPER):
         eliminate_super(x_out, base)
-        if base == 0:
-            arrive(cols_first)
-            cols_sum[...] = combine(cols_ref, cols_got, "col", cols_count)
-            cols_mine = pl.ds(my_col * cols_count, cols_count)
-            cols_out[cols_mine, :] = cols_sum[...]
-            cols_second = send_all("col", lambda d: cols_sum, lambda d: cols_out.at[cols_mine])
     arrive(rows_second)
     arrive(cols_second)
     for copies in (
@@ -304,6 +318,8 @@
     ):
         for copy in copies:
             copy.wait_send()
+    for store in stores:
+        store.wait()
 
 
 def tile_kernel(
@@ -311,7 +327,7 @@
     prec_ref, feat_r_ref, feat_c_ref, feat_p_ref, cols_ref, rows_ref, x_ref, mean_p_ref,
     stats_ref, y_ref, mean_ref,
     out_ref, mean_out,
-    solved, solved_high, solved_low, inverse_high, inverse_low, head,
+    solved, solved_parts, inverse_high, inverse_low, head,
 ):
     step = pl.program_id(0)
     in_row = info[2] == 1
@@ -329,7 +345,10 @@
         joined = keep * rows_ref[...].astype(F32) + gram_scale * dot(feat_p_ref[...], feat_c_ref[...], NT)
         result = dot_split((high, low), split_two(joined), NN)
         solved[...] = result
-        solved_high[...], solved_low[...] = split_two(result)
+        result_high, result_low = split_two(result)
+        solved_parts[:PB, :] = result_high
+        solved_parts[PB : 2 * PB, :] = result_high
+        solved_parts[2 * PB :, :] = result_low
         fit = dot(y_ref[...], feat_p_ref[...], NT)
         head[...] = dot(keep * mean_p_ref[...] + mean_scale * fit, inverse, NT, HIGHEST)
 
@@ -338,12 +357,11 @@
     wide = dot_split(split_two(piece), (inverse_high[...], inverse_low[...]), NT)
     wide_high, wide_low = split_two(wide)
     tile = keep * prec_ref[...] + gram_scale * dot(feat_r, feat_c_ref[...], NT)
-    out_ref[...] = tile - dot_split(
-        (wide_high, wide_low), (solved_high[...], solved_low[...]), NN
-    )
+    wide_parts = jnp.concatenate([wide_high, wide_low, wide_high], axis=1)
+    out_ref[...] = tile - dot(wide_parts, solved_parts[...], NN)
     fit = dot(y_ref[...], feat_r, NT)
     mean_next = (
-        keep * mean_ref[...] + mean_scale * fit[:1, :] - dot(head[...], wide, NT, HIGHEST)[:1, :]
+        keep * mean_ref[...] + mean_scale * fit[:1, :] - dot_split(split_two(head[...]), (wide_high, wide_low), NT)[:1, :]
     )
     mean_out[...] = mean_next
     col0 = pl.multiple_of(info[1] * PB, PB)
@@ -428,7 +446,7 @@
             shape((diag_rows, PB), F32),
             shape((PB, width), F32),
         ],
-        compiler_params=pltpu.CompilerParams(vmem_limit_bytes=40 << 20),
+        compiler_params=pltpu.CompilerParams(vmem_limit_bytes=VMEM),
         name="prep",
     )(
         info, picks.reshape(1, batch), pool, targets.reshape(1, -1),
@@ -439,8 +457,8 @@
     rows_count = PB // n_rows
     moved = pl.pallas_call(
         functools.partial(move_kernel, n_rows, n_cols),
-        in_specs=[whole()] * 7,
-        out_specs=[whole()] * 9,
+        in_specs=[whole()] * 5 + [whole(pl.ANY), whole()],
+        out_specs=[whole(pl.ANY)] * 2 + [whole()] * 7,
         out_shape=[
             shape((tile_rows, n_batch), BF16),
             shape((tile_cols, n_batch), BF16),
@@ -453,6 +471,9 @@
             shape((SUB, n_batch), BF16),
         ],
         scratch_shapes=[
+            pltpu.VMEM(inducing.shape, F32),
+            pltpu.VMEM((tile_rows, n_batch), BF16),
+            pltpu.VMEM((tile_cols, n_batch), BF16),
             pltpu.VMEM((n_cols, n_rows, batch, width + LANES), BF16),
             pltpu.VMEM((n_rows - 1, diag_count, PB), F32),
             pltpu.VMEM((diag_count, PB), F32),
@@ -465,9 +486,10 @@
             pltpu.VMEM((n_batch, 2 * width), BF16),
             pltpu.SemaphoreType.DMA((sems,)),
             pltpu.SemaphoreType.DMA((sems,)),
+            pltpu.SemaphoreType.DMA((3,)),
         ],
         compiler_params=pltpu.CompilerParams(
-            collective_id=0, has_side_effects=True, vmem_limit_bytes=56 << 20
+            collective_id=0, has_side_effects=True, vmem_limit_bytes=VMEM
         ),
         name="move",
     )(points, xs, cols, rows, diag, inducing, inv_sq_lengths.reshape(1, width))
@@ -497,15 +519,14 @@
             ],
             scratch_shapes=[
                 pltpu.VMEM((PB, tile_cols), F32),
-                pltpu.VMEM((PB, tile_cols), BF16),
-                pltpu.VMEM((PB, tile_cols), BF16),
+                pltpu.VMEM((3 * PB, tile_cols), BF16),
                 pltpu.VMEM((PB, PB), BF16),
                 pltpu.VMEM((PB, PB), BF16),
                 pltpu.VMEM((SUB, PB), F32),
             ],
         ),
         out_shape=[shape((tile_rows, tile_cols), F32), shape((1, tile_rows), F32)],
-        compiler_params=pltpu.CompilerParams(vmem_limit_bytes=56 << 20),
+        compiler_params=pltpu.CompilerParams(vmem_limit_bytes=VMEM),
         name="tile",
     )(
         info, prec_old, feat_r, feat_c, feat_p, got_cols, got_rows, x, mean_p, stats, y, mean_row,

time: 80.8 us -> 73.1 us (0.905)
  the two profiles are of different devices: /device:TPU:0 before, /device:TPU:1 now
where the time goes in v2:
time: 73.1 us; the launch traced here: 72.8 us
  Pallas kernels  70.9 us (97%)
  between operations  1.33 us (2%)
    pallas_call x1, Pallas kernels, local(): pl.pallas_call(functools.partial(move_kernel, n_rows, n_cols), in_specs=[...  50.5 us
    pallas_call x1, Pallas kernels, local(): pl.pallas_call(tile_kernel, grid_spec=pltpu.PrefetchScalarGridSpec(num_sc...  16.1 us
    pallas_call x1, Pallas kernels, local(): pl.pallas_call(prep_kernel, grid_spec=pltpu.PrefetchScalarGridSpec(num_sc...  4.31 us

profile of v2, /device:TPU:1, one launch (start us, length us, event | category | flops | bytes accessed | tf_op | source)
XLA Modules:
  0.0 72.8 jit_solution(8018459009783583112)
XLA Ops:
  1.3 0.6 stack.27.info
  1.9 4.3 %prep.1 = (bf16[16,256]{1,0:T(8,128)(2,1)}, bf16[1024,256]{1,0:T(8,128)(2,1)}, bf16[256,2048]{1,0:T(8,128)(2,1)}, f32[320,256]{1,0:T(8,128)}, f32[256,128]{1,0:T(8,128)}) custom-call(s32[5]{0:T(128)} %stack.27.info, s32[1,16]{1,0:T(1,128)} %bitcast.16, bf16[128,128]{1,0:T(8,128)(2,1)} %pool_ref.1, bf16[1,128]{1,0:T(2,128)(2,1)} %bitcast.17, ...), custom_call_target="tpu_custom_call" | custom-call | tf_op jit(solution)/shard_map/prep/pallas_call | solution.py:419
  6.3 50.5 %move.1 = (bf16[1024,512]{1,0:T(8,128)(2,1)}, bf16[2048,512]{1,0:T(8,128)(2,1)}, bf16[256,512]{1,0:T(8,128)(2,1)}, bf16[1024,256]{1,0:T(8,128)(2,1)}, bf16[256,2...) custom-call(f32[256,128]{1,0:T(8,128)} %get-tuple-element.18.points_r, ...), custom_call_target="tpu_custom_call" | custom-call | tf_op jit(solution)/shard_map/move/pallas_call | solution.py:458
  56.8 16.1 %tile.1 = (f32[1024,2048]{1,0:T(8,128)}, f32[1,1024]{1,0:T(1,128)}) custom-call(s32[5]{0:T(128)} %stack.27.info, f32[1024,2048]{1,0:T(8,128)} %prec_ref.1, bf16[1024,512]{1,0:T(8,128)(2,1)} %get-tuple-element.23.feat_r_ref, bf16[2048,512]{1,0:T(8,128)(2,1)} %get-tuple-element.24.feat_c_ref, bf16[256,512]{1,0:T(8,128)(2,1)} %get-tuple-element.25.feat_p_ref, ...), custom_call_target="tpu_custom_call" | custom-call | tf_op jit(solution)/shard_map/tile/pallas_call | solution.py:498

commit v3 on v2

--- a/solution.py
+++ b/solution.py
@@ -12,6 +12,8 @@
 EPSILON = 1e-05
 SUPER = 64
 SUB = 8
+WIDE = 16
+CHUNK = 512
 LANES = 128
 VMEM = 62 << 20
 F32 = jnp.float32
@@ -82,36 +84,40 @@
 def eliminate_super(x_ref, base):
     sub_ids = lax.broadcasted_iota(jnp.int32, (SUB, LANES), 0)
     groups = SUPER // SUB
+    per = WIDE // SUB
     size = x_ref.shape[0]
-    for step in range(groups):
-        col0 = base + step * SUB
-        lane_tiles = [t for t in range(size // LANES) if (t + 1) * LANES > col0]
-        lane_tiles += [size // LANES + t for t in range(size // LANES) if t * LANES < col0 + SUB]
-        rows = {
-            g: x_ref[base + g * SUB : base + (g + 1) * SUB, col0 : col0 + SUB]
-            for g in range(step, groups)
-        }
-        column = {
-            g: [jnp.broadcast_to(rows[g][:, k : k + 1], (SUB, LANES)) for k in range(SUB)]
-            for g in rows
-        }
-        square = {
-            (m, k): jnp.broadcast_to(column[step][k][m : m + 1, :], (SUB, LANES))
-            for k in range(SUB)
-            for m in range(k + 1)
-        }
+    tiles_of = size // LANES
+    after = base + SUPER
+    for step in range(SUPER // WIDE):
+        col0 = base + step * WIDE
+        first = step * per
+        lane_tiles = [t for t in range(tiles_of) if (t + 1) * LANES > col0]
+        lane_tiles += [tiles_of + t for t in range(tiles_of) if t * LANES < col0 + WIDE]
+        column = {}
+        for g in range(first, groups):
+            piece = x_ref[base + g * SUB : base + (g + 1) * SUB, col0 : col0 + WIDE]
+            column[g] = [jnp.broadcast_to(piece[:, k : k + 1], (SUB, LANES)) for k in range(WIDE)]
+        square = {}
+        for k in range(WIDE):
+            for m in range(k + 1):
+                source = column[first + m // SUB][k]
+                square[m, k] = jnp.broadcast_to(
+                    source[m % SUB : m % SUB + 1, :], (SUB, LANES)
+                )
         scale = []
         below = {}
-        for k in range(SUB):
+        for k in range(WIDE):
             scale.append(lax.rsqrt(square[k, k]))
-            for j in range(k + 1, SUB):
+            for j in range(k + 1, WIDE):
                 below[j, k] = square[k, j] * scale[k]
-            for m in range(k + 1, SUB):
-                for j in range(m, SUB):
+            for m in range(k + 1, WIDE):
+                for j in range(m, WIDE):
                     square[m, j] = square[m, j] - below[m, k] * below[j, k]
         factor_cols = {}
-        for g in rows:
-            for k in range(SUB):
+        for g in range(first, groups):
+            for k in range(WIDE):
+                if g - first < k // SUB:
+                    continue
                 value = column[g][k]
                 for m in range(k):
                     value = value - factor_cols[g, m] * below[k, m]
@@ -119,27 +125,35 @@
         for t in lane_tiles:
             lanes = slice(t * LANES, (t + 1) * LANES)
             tiles = {
-                g: x_ref[base + g * SUB : base + (g + 1) * SUB, lanes] for g in range(step, groups)
+                g: x_ref[base + g * SUB : base + (g + 1) * SUB, lanes]
+                for g in range(first, groups)
             }
-            for k in range(SUB):
-                pivot_row = jnp.broadcast_to(tiles[step][k : k + 1, :], (SUB, LANES)) * scale[k]
-                mine = tiles[step] - jnp.where(sub_ids > k, factor_cols[step, k], 0.0) * pivot_row
-                tiles[step] = jnp.where(sub_ids == k, pivot_row, mine)
-                for g in range(step + 1, groups):
+            for k in range(WIDE):
+                own = first + k // SUB
+                at = k % SUB
+                pivot_row = jnp.broadcast_to(tiles[own][at : at + 1, :], (SUB, LANES)) * scale[k]
+                mine = tiles[own] - jnp.where(sub_ids > at, factor_cols[own, k], 0.0) * pivot_row
+                tiles[own] = jnp.where(sub_ids == at, pivot_row, mine)
+                for g in range(own + 1, groups):
                     tiles[g] = tiles[g] - factor_cols[g, k] * pivot_row
             for g in tiles:
                 x_ref[base + g * SUB : base + (g + 1) * SUB, lanes] = tiles[g]
-    after = base + SUPER
     if after < size:
-        done = x_ref[base:after, :]
-        x_ref[after:, :] = x_ref[after:, :] - dot(done[:, after:size], done, TN, HIGHEST)
+        done = x_ref[base:after, after:size]
+        for low, high in (
+            (after // LANES * LANES, size),
+            (size, size + -(-after // LANES) * LANES),
+        ):
+            x_ref[after:, low:high] = x_ref[after:, low:high] - dot(
+                done, x_ref[base:after, low:high], TN, HIGHEST
+            )
 
 
 def move_kernel(
     n_rows, n_cols,
     points_ref, xs_ref, cols_ref, rows_ref, diag_ref, inducing_ref, weights_ref,
     feat_r_out, feat_c_out, feat_p_out, cols_out, rows_out, x_out, mean_out, stats_out, y_out,
-    points_v, feat_r, feat_c,
+    points_c, points_r, feat_r, feat_c, trace_all,
     all_x, diag_got, diag_sum, diag_col, diag_all, cols_got, cols_sum, rows_got, rows_sum, twice,
     send_sem, recv_sem, local_sem,
 ):
@@ -177,8 +191,19 @@
         for copy in copies:
             copy.wait_recv()
 
-    load_points = pltpu.make_async_copy(inducing_ref, points_v, local_sem.at[0])
-    load_points.start()
+    tile_rows = feat_r.shape[0]
+    tile_cols = feat_c.shape[0]
+    points_count = inducing_ref.shape[0]
+    loads = [
+        pltpu.make_async_copy(
+            inducing_ref.at[pl.ds(my_col * tile_cols, tile_cols)], points_c, local_sem.at[0]
+        ),
+        pltpu.make_async_copy(
+            inducing_ref.at[pl.ds(my_row * tile_rows, tile_rows)], points_r, local_sem.at[3]
+        ),
+    ]
+    for load in loads:
+        load.start()
 
     barrier = pltpu.get_barrier_semaphore()
     for axis in ("row", "col"):
@@ -212,15 +237,9 @@
     )
     arrive(xs_first)
     xs_second = send_all("col", lambda d: all_x.at[my_col], lambda d: all_x.at[my_col])
-    cols_first = send_all(
-        "col", slices(cols_count, cols_ref, "col"), lambda d: cols_got.at[d - 1]
-    )
     arrive(diag_first)
     diag_sum[...] = combine(diag_ref, diag_got, "row", diag_count)
     diag_second = send_all("col", lambda d: diag_sum, lambda d: diag_col.at[d - 1])
-    rows_first = send_all(
-        "row", slices(rows_count, rows_ref, "row"), lambda d: rows_got.at[d - 1]
-    )
     arrive(xs_second)
 
     width = inducing_ref.shape[1]
@@ -236,70 +255,62 @@
     samples_f = samples.astype(F32)
     samples_sq = dot(jnp.broadcast_to(weights, (SUB, width)), samples_f * samples_f, NT, HIGHEST)[:1, :]
 
-    tile_rows = feat_r.shape[0]
-    tile_cols = feat_c.shape[0]
-    points_count = inducing_ref.shape[0]
-
     def features_of(points):
         return feature_block(points, weights, twice[...], samples_sq)
 
     step_rows = min(2 * PB, tile_rows, tile_cols)
 
-    def trace_step(index, total):
-        start = pl.multiple_of(index * step_rows, step_rows)
-        exact = features_of(points_v[pl.ds(start, step_rows), :])
-        block = exact.astype(BF16)
-
-        @pl.when(start // tile_rows == my_row)
-        def _():
-            feat_r[pl.ds(pl.multiple_of(lax.rem(start, tile_rows), step_rows), step_rows), :] = block
-
-        @pl.when(start // tile_cols == my_col)
-        def _():
-            feat_c[pl.ds(pl.multiple_of(lax.rem(start, tile_cols), step_rows), step_rows), :] = block
-
+    def col_step(index, total):
+        rows = pl.ds(pl.multiple_of(index * step_rows, step_rows), step_rows)
+        exact = features_of(points_c[rows, :])
+        feat_c[rows, :] = exact.astype(BF16)
         return total + jnp.sum((exact * exact).reshape(step_rows // SUB, SUB, n_batch), axis=0)
 
-    load_points.wait()
-    partial = jnp.zeros((SUB, n_batch), F32)
-    quarter = points_count // step_rows // 4
-    for part in range(4):
-        partial = lax.fori_loop(part * quarter, (part + 1) * quarter, trace_step, partial)
-        if part == 1:
-            arrive(diag_second)
-            total = diag_sum[...]
-            for distance in range(1, n_cols):
-                total = total + diag_col[distance - 1]
-            diag_all[diag_mine, :] = total
-            diag_third = send_all(
-                "row", lambda d: diag_all.at[diag_mine], lambda d: diag_all.at[diag_mine]
-            )
-        if part == 2:
-            arrive(cols_first)
-            cols_sum[...] = combine(cols_ref, cols_got, "col", cols_count)
-            cols_out[cols_mine, :] = cols_sum[...]
-            cols_second = send_all("col", lambda d: cols_sum, lambda d: cols_out.at[cols_mine])
+    def row_step(index, carry):
+        rows = pl.ds(pl.multiple_of(index * step_rows, step_rows), step_rows)
+        feat_r[rows, :] = features_of(points_r[rows, :]).astype(BF16)
+        return carry
+
+    loads[0].wait()
+    partial = lax.fori_loop(
+        0, tile_cols // step_rows, col_step, jnp.zeros((SUB, n_batch), F32)
+    )
+    trace_all[my_col] = jnp.broadcast_to(jnp.sum(partial, keepdims=True), (SUB, LANES))
+    trace_sent = send_all("col", lambda d: trace_all.at[my_col], lambda d: trace_all.at[my_col])
+    arrive(diag_second)
+    total = diag_sum[...]
+    for distance in range(1, n_cols):
+        total = total + diag_col[distance - 1]
+    diag_all[diag_mine, :] = total
+    diag_third = send_all("row", lambda d: diag_all.at[diag_mine], lambda d: diag_all.at[diag_mine])
+    cols_first = send_all(
+        "col", slices(cols_count, cols_ref, "col"), lambda d: cols_got.at[d - 1]
+    )
+    rows_first = send_all(
+        "row", slices(rows_count, rows_ref, "row"), lambda d: rows_got.at[d - 1]
+    )
+    loads[1].wait()
+    lax.fori_loop(0, tile_rows // step_rows, row_step, 0)
     stores = [
         pltpu.make_async_copy(feat_r, feat_r_out, local_sem.at[1]),
         pltpu.make_async_copy(feat_c, feat_c_out, local_sem.at[2]),
     ]
     for store in stores:
         store.start()
-    trace_scale = jnp.sum(partial, keepdims=True) / points_count
+    feat_p = features_of(points_ref[...]).astype(BF16)
+    feat_p_out[...] = feat_p
+    gram_p = dot(feat_p, feat_p, NT)
+    arrive(trace_sent)
+    trace_sum = trace_all[0]
+    for col in range(1, n_cols):
+        trace_sum = trace_sum + trace_all[col]
+    trace_scale = trace_sum[:1, :1] / points_count
     gram_scale = RATE / trace_scale
     mean_scale = RATE * lax.rsqrt(trace_scale * (power / n_batch + EPSILON))
     stats_out[0:1, :] = jnp.broadcast_to(gram_scale, (1, LANES))
     stats_out[1:2, :] = jnp.broadcast_to(mean_scale, (1, LANES))
     stats_out[2:, :] = jnp.zeros((SUB - 2, LANES), F32)
 
-    arrive(rows_first)
-    rows_sum[...] = combine(rows_ref, rows_got, "row", rows_count)
-    rows_out[rows_mine, :] = rows_sum[...]
-    rows_second = send_all("row", lambda d: rows_sum, lambda d: rows_out.at[rows_mine])
-
-    feat_p = features_of(points_ref[...]).astype(BF16)
-    feat_p_out[...] = feat_p
-    gram_p = dot(feat_p, feat_p, NT)
     arrive(diag_third)
     mean_out[...] = diag_all[PB : PB + SUB, :]
     x_out[:, :PB] = (1.0 - RATE) * diag_all[:PB, :] + gram_scale * gram_p
@@ -310,10 +321,19 @@
     )
     for base in range(0, PB, SUPER):
         eliminate_super(x_out, base)
+        if base == SUPER:
+            arrive(cols_first)
+            cols_sum[...] = combine(cols_ref, cols_got, "col", cols_count)
+            cols_out[cols_mine, :] = cols_sum[...]
+            cols_second = send_all("col", lambda d: cols_sum, lambda d: cols_out.at[cols_mine])
+            arrive(rows_first)
+            rows_sum[...] = combine(rows_ref, rows_got, "row", rows_count)
+            rows_out[rows_mine, :] = rows_sum[...]
+            rows_second = send_all("row", lambda d: rows_sum, lambda d: rows_out.at[rows_mine])
     arrive(rows_second)
     arrive(cols_second)
     for copies in (
-        xs_first, xs_second, diag_first, diag_second, diag_third,
+        xs_first, xs_second, trace_sent, diag_first, diag_second, diag_third,
         rows_first, rows_second, cols_first, cols_second,
     ):
         for copy in copies:
@@ -356,9 +376,13 @@
     piece = keep * cols_ref[...].astype(F32) + gram_scale * dot(feat_r, feat_p_ref[...], NT)
     wide = dot_split(split_two(piece), (inverse_high[...], inverse_low[...]), NT)
     wide_high, wide_low = split_two(wide)
-    tile = keep * prec_ref[...] + gram_scale * dot(feat_r, feat_c_ref[...], NT)
     wide_parts = jnp.concatenate([wide_high, wide_low, wide_high], axis=1)
-    out_ref[...] = tile - dot(wide_parts, solved_parts[...], NN)
+    for low in range(0, prec_ref.shape[1], CHUNK):
+        lanes = slice(low, low + CHUNK)
+        gram = dot(feat_r, feat_c_ref[lanes, :], NT)
+        out_ref[:, lanes] = (keep * prec_ref[:, lanes] + gram_scale * gram) - dot(
+            wide_parts, solved_parts[:, lanes], NN
+        )
     fit = dot(y_ref[...], feat_r, NT)
     mean_next = (
         keep * mean_ref[...] + mean_scale * fit[:1, :] - dot_split(split_two(head[...]), (wide_high, wide_low), NT)[:1, :]
@@ -452,7 +476,7 @@
         info, picks.reshape(1, batch), pool, targets.reshape(1, -1),
         prec_old, prec_old, prec_old, mean_row, inducing,
     )
-    sems = 5 * (n_rows - 1) + 4 * (n_cols - 1)
+    sems = 5 * (n_rows - 1) + 5 * (n_cols - 1)
     cols_count = tile_rows // n_cols
     rows_count = PB // n_rows
     moved = pl.pallas_call(
@@ -471,9 +495,11 @@
             shape((SUB, n_batch), BF16),
         ],
         scratch_shapes=[
-            pltpu.VMEM(inducing.shape, F32),
+            pltpu.VMEM((tile_cols, width), F32),
+            pltpu.VMEM((tile_rows, width), F32),
             pltpu.VMEM((tile_rows, n_batch), BF16),
             pltpu.VMEM((tile_cols, n_batch), BF16),
+            pltpu.VMEM((n_cols, SUB, LANES), F32),
             pltpu.VMEM((n_cols, n_rows, batch, width + LANES), BF16),
             pltpu.VMEM((n_rows - 1, diag_count, PB), F32),
             pltpu.VMEM((diag_count, PB), F32),
@@ -486,7 +512,7 @@
             pltpu.VMEM((n_batch, 2 * width), BF16),
             pltpu.SemaphoreType.DMA((sems,)),
             pltpu.SemaphoreType.DMA((sems,)),
-            pltpu.SemaphoreType.DMA((3,)),
+            pltpu.SemaphoreType.DMA((4,)),
         ],
         compiler_params=pltpu.CompilerParams(
             collective_id=0, has_side_effects=True, vmem_limit_bytes=VMEM

time: 73.1 us -> 74.3 us (1.016)
  Pallas kernels: 70.9 us -> 72 us
    pallas_call x1, Pallas kernels: 50.5 us -> 51.6 us  [local(): pl.pallas_call(functools.partial(move_kernel, n_rows, n_cols), in_specs=[...]
where the time goes in v3:
time: 74.3 us; the launch traced here: 74 us
  Pallas kernels  72 us (97%)
  between operations  1.33 us (2%)
    pallas_call x1, Pallas kernels, local(): pl.pallas_call(functools.partial(move_kernel, n_rows, n_cols), in_specs=[...  51.6 us
    pallas_call x1, Pallas kernels, local(): pl.pallas_call(tile_kernel, grid_spec=pltpu.PrefetchScalarGridSpec(num_sc...  16.1 us
    pallas_call x1, Pallas kernels, local(): pl.pallas_call(prep_kernel, grid_spec=pltpu.PrefetchScalarGridSpec(num_sc...  4.31 us

profile of v3, /device:TPU:1, one launch (start us, length us, event | category | flops | bytes accessed | tf_op | source)
XLA Modules:
  0.0 74.0 jit_solution(9062565426924526709)
XLA Ops:
  1.3 0.6 stack.27.info
  1.9 4.3 %prep.1 = (bf16[16,256]{1,0:T(8,128)(2,1)}, bf16[1024,256]{1,0:T(8,128)(2,1)}, bf16[256,2048]{1,0:T(8,128)(2,1)}, f32[320,256]{1,0:T(8,128)}, f32[256,128]{1,0:T(8,128)}) custom-call(s32[5]{0:T(128)} %stack.27.info, s32[1,16]{1,0:T(1,128)} %bitcast.16, bf16[128,128]{1,0:T(8,128)(2,1)} %pool_ref.1, bf16[1,128]{1,0:T(2,128)(2,1)} %bitcast.17, ...), custom_call_target="tpu_custom_call" | custom-call | tf_op jit(solution)/shard_map/prep/pallas_call | solution.py:443
  6.3 51.6 %move.1 = (bf16[1024,512]{1,0:T(8,128)(2,1)}, bf16[2048,512]{1,0:T(8,128)(2,1)}, bf16[256,512]{1,0:T(8,128)(2,1)}, bf16[1024,256]{1,0:T(8,128)(2,1)}, bf16[256,2...) custom-call(f32[256,128]{1,0:T(8,128)} %get-tuple-element.18.points_r, ...), custom_call_target="tpu_custom_call" | custom-call | tf_op jit(solution)/shard_map/move/pallas_call | solution.py:482
  57.9 16.1 %tile.1 = (f32[1024,2048]{1,0:T(8,128)}, f32[1,1024]{1,0:T(1,128)}) custom-call(s32[5]{0:T(128)} %stack.27.info, f32[1024,2048]{1,0:T(8,128)} %prec_ref.1, bf16[1024,512]{1,0:T(8,128)(2,1)} %get-tuple-element.23.feat_r_ref, bf16[2048,512]{1,0:T(8,128)(2,1)} %get-tuple-element.24.feat_c_ref, bf16[256,512]{1,0:T(8,128)(2,1)} %get-tuple-element.25.feat_p_ref, ...), custom_call_target="tpu_custom_call" | custom-call | tf_op jit(solution)/shard_map/tile/pallas_call | solution.py:524

commit v4 on v3

--- a/solution.py
+++ b/solution.py
@@ -12,8 +12,9 @@
 EPSILON = 1e-05
 SUPER = 64
 SUB = 8
-WIDE = 16
+WIDE = 8
 CHUNK = 512
+PREP = 4
 LANES = 128
 VMEM = 62 << 20
 F32 = jnp.float32
@@ -46,6 +47,23 @@
 ):
     in_row = info[2] == 1
     in_col = info[3] == 1
+    zero = jnp.float32(0.0)
+    cols_out[...] = jnp.where(in_col, cols_ref[...], zero).astype(BF16)
+    rows_out[...] = jnp.where(in_row, rows_ref[...], zero).astype(BF16)
+    first = pl.program_id(0) == 0
+
+    @pl.when(first)
+    def _():
+        prep_small(
+            in_row, in_col, picks_ref, pool_ref, targets_ref, diag_ref, mean_ref, points_ref,
+            xs_out, diag_out, points_out,
+        )
+
+
+def prep_small(
+    in_row, in_col, picks_ref, pool_ref, targets_ref, diag_ref, mean_ref, points_ref,
+    xs_out, diag_out, points_out,
+):
     pool_count = pool_ref.shape[0]
     batch = picks_ref.shape[1]
     ids = lax.broadcasted_iota(jnp.int32, (pool_count, batch), 0)
@@ -63,8 +81,6 @@
     xs_out[:, :width] = samples.astype(BF16)
     xs_out[:, width:] = jnp.broadcast_to(values, (batch, LANES)).astype(BF16)
     zero = jnp.float32(0.0)
-    cols_out[...] = jnp.where(in_col, cols_ref[...], zero).astype(BF16)
-    rows_out[...] = jnp.where(in_row, rows_ref[...], zero).astype(BF16)
     points_out[...] = points_ref[...]
     both = jnp.logical_and(in_row, in_col)
     diag_out[:PB, :] = jnp.where(both, diag_ref[...], zero)
@@ -237,9 +253,15 @@
     )
     arrive(xs_first)
     xs_second = send_all("col", lambda d: all_x.at[my_col], lambda d: all_x.at[my_col])
+    cols_first = send_all(
+        "col", slices(cols_count, cols_ref, "col"), lambda d: cols_got.at[d - 1]
+    )
     arrive(diag_first)
     diag_sum[...] = combine(diag_ref, diag_got, "row", diag_count)
     diag_second = send_all("col", lambda d: diag_sum, lambda d: diag_col.at[d - 1])
+    rows_first = send_all(
+        "row", slices(rows_count, rows_ref, "row"), lambda d: rows_got.at[d - 1]
+    )
     arrive(xs_second)
 
     width = inducing_ref.shape[1]
@@ -283,12 +305,6 @@
         total = total + diag_col[distance - 1]
     diag_all[diag_mine, :] = total
     diag_third = send_all("row", lambda d: diag_all.at[diag_mine], lambda d: diag_all.at[diag_mine])
-    cols_first = send_all(
-        "col", slices(cols_count, cols_ref, "col"), lambda d: cols_got.at[d - 1]
-    )
-    rows_first = send_all(
-        "row", slices(rows_count, rows_ref, "row"), lambda d: rows_got.at[d - 1]
-    )
     loads[1].wait()
     lax.fori_loop(0, tile_rows // step_rows, row_step, 0)
     stores = [
@@ -321,7 +337,7 @@
     )
     for base in range(0, PB, SUPER):
         eliminate_super(x_out, base)
-        if base == SUPER:
+        if base == 0:
             arrive(cols_first)
             cols_sum[...] = combine(cols_ref, cols_got, "col", cols_count)
             cols_out[cols_mine, :] = cols_sum[...]
@@ -444,21 +460,21 @@
         prep_kernel,
         grid_spec=pltpu.PrefetchScalarGridSpec(
             num_scalar_prefetch=1,
-            grid=(1,),
+            grid=(PREP,),
             in_specs=[
                 full(1, batch),
                 full(*pool.shape),
                 full(1, pool.shape[0]),
-                pl.BlockSpec((tile_rows, PB), lambda i, info: (0, info[1])),
-                pl.BlockSpec((PB, tile_cols), lambda i, info: (info[0], 0)),
+                pl.BlockSpec((tile_rows // PREP, PB), lambda i, info: (i, info[1])),
+                pl.BlockSpec((PB, tile_cols // PREP), lambda i, info: (info[0], i)),
                 pl.BlockSpec((PB, PB), lambda i, info: (info[0], info[1])),
                 pl.BlockSpec((1, PB), lambda i, info: (0, info[0])),
                 pl.BlockSpec((PB, width), lambda i, info: (info[4], 0)),
             ],
             out_specs=[
                 full(batch, width + LANES),
-                full(tile_rows, PB),
-                full(PB, tile_cols),
+                pl.BlockSpec((tile_rows // PREP, PB), lambda i, info: (i, 0)),
+                pl.BlockSpec((PB, tile_cols // PREP), lambda i, info: (0, i)),
                 full(diag_rows, PB),
                 full(PB, width),
             ],

time: 74.3 us -> 79.5 us (1.070)
  Pallas kernels: 72 us -> 77.2 us
    pallas_call x1, Pallas kernels: 51.6 us -> 55.8 us  [local(): pl.pallas_call(functools.partial(move_kernel, n_rows, n_cols), in_specs=[...]
    pallas_call x1, Pallas kernels: 4.31 us -> 5.27 us  [local(): pl.pallas_call(prep_kernel, grid_spec=pltpu.PrefetchScalarGridSpec(num_sc...]
where the time goes in v4:
time: 79.5 us; the launch traced here: 79.2 us
  Pallas kernels  77.2 us (97%)
  between operations  1.33 us (2%)
    pallas_call x1, Pallas kernels, local(): pl.pallas_call(functools.partial(move_kernel, n_rows, n_cols), in_specs=[...  55.8 us
    pallas_call x1, Pallas kernels, local(): pl.pallas_call(tile_kernel, grid_spec=pltpu.PrefetchScalarGridSpec(num_sc...  16.1 us
    pallas_call x1, Pallas kernels, local(): pl.pallas_call(prep_kernel, grid_spec=pltpu.PrefetchScalarGridSpec(num_sc...  5.27 us

profile of v4, /device:TPU:1, one launch (start us, length us, event | category | flops | bytes accessed | tf_op | source)
XLA Modules:
  0.0 79.2 jit_solution(8454430395422360513)
XLA Ops:
  1.3 0.6 stack.27.info
  1.9 5.3 %prep.1 = (bf16[16,256]{1,0:T(8,128)(2,1)}, bf16[1024,256]{1,0:T(8,128)(2,1)}, bf16[256,2048]{1,0:T(8,128)(2,1)}, f32[320,256]{1,0:T(8,128)}, f32[256,128]{1,0:T(8,128)}) custom-call(s32[5]{0:T(128)} %stack.27.info, s32[1,16]{1,0:T(1,128)} %bitcast.16, bf16[128,128]{1,0:T(8,128)(2,1)} %pool_ref.1, bf16[1,128]{1,0:T(2,128)(2,1)} %bitcast.17, ...), custom_call_target="tpu_custom_call" | custom-call | tf_op jit(solution)/shard_map/prep/pallas_call | solution.py:459
  7.2 55.8 %move.1 = (bf16[1024,512]{1,0:T(8,128)(2,1)}, bf16[2048,512]{1,0:T(8,128)(2,1)}, bf16[256,512]{1,0:T(8,128)(2,1)}, bf16[1024,256]{1,0:T(8,128)(2,1)}, bf16[256,2...) custom-call(f32[256,128]{1,0:T(8,128)} %get-tuple-element.18.points_r, ...), custom_call_target="tpu_custom_call" | custom-call | tf_op jit(solution)/shard_map/move/pallas_call | solution.py:498
  63.1 16.1 %tile.1 = (f32[1024,2048]{1,0:T(8,128)}, f32[1,1024]{1,0:T(1,128)}) custom-call(s32[5]{0:T(128)} %stack.27.info, f32[1024,2048]{1,0:T(8,128)} %prec_ref.1, bf16[1024,512]{1,0:T(8,128)(2,1)} %get-tuple-element.23.feat_r_ref, bf16[2048,512]{1,0:T(8,128)(2,1)} %get-tuple-element.24.feat_c_ref, bf16[256,512]{1,0:T(8,128)(2,1)} %get-tuple-element.25.feat_p_ref, ...), custom_call_target="tpu_custom_call" | custom-call | tf_op jit(solution)/shard_map/tile/pallas_call | solution.py:540

commit v5 on v3

--- a/solution.py
+++ b/solution.py
@@ -12,7 +12,7 @@
 EPSILON = 1e-05
 SUPER = 64
 SUB = 8
-WIDE = 16
+WIDE = 8
 CHUNK = 512
 LANES = 128
 VMEM = 62 << 20
@@ -321,7 +321,7 @@
     )
     for base in range(0, PB, SUPER):
         eliminate_super(x_out, base)
-        if base == SUPER:
+        if base == 0:
             arrive(cols_first)
             cols_sum[...] = combine(cols_ref, cols_got, "col", cols_count)
             cols_out[cols_mine, :] = cols_sum[...]

time: 74.3 us -> 75.3 us (1.013); the launches traced: 74 us -> 73.8 us
  no operation moved by 1% of the time
where the time goes in v5:
time: 75.3 us; the launch traced here: 73.8 us
  Pallas kernels  71.9 us (95%)
  between operations  1.33 us (2%)
    pallas_call x1, Pallas kernels, local(): pl.pallas_call(functools.partial(move_kernel, n_rows, n_cols), in_specs=[...  51.6 us
    pallas_call x1, Pallas kernels, local(): pl.pallas_call(tile_kernel, grid_spec=pltpu.PrefetchScalarGridSpec(num_sc...  15.9 us
    pallas_call x1, Pallas kernels, local(): pl.pallas_call(prep_kernel, grid_spec=pltpu.PrefetchScalarGridSpec(num_sc...  4.31 us

profile of v5, /device:TPU:1, one launch (start us, length us, event | category | flops | bytes accessed | tf_op | source)
XLA Modules:
  0.0 73.8 jit_solution(1269817735413155985)
XLA Ops:
  1.3 0.6 stack.27.info
  1.9 4.3 %prep.1 = (bf16[16,256]{1,0:T(8,128)(2,1)}, bf16[1024,256]{1,0:T(8,128)(2,1)}, bf16[256,2048]{1,0:T(8,128)(2,1)}, f32[320,256]{1,0:T(8,128)}, f32[256,128]{1,0:T(8,128)}) custom-call(s32[5]{0:T(128)} %stack.27.info, s32[1,16]{1,0:T(1,128)} %bitcast.16, bf16[128,128]{1,0:T(8,128)(2,1)} %pool_ref.1, bf16[1,128]{1,0:T(2,128)(2,1)} %bitcast.17, ...), custom_call_target="tpu_custom_call" | custom-call | tf_op jit(solution)/shard_map/prep/pallas_call | solution.py:443
  6.3 51.6 %move.1 = (bf16[1024,512]{1,0:T(8,128)(2,1)}, bf16[2048,512]{1,0:T(8,128)(2,1)}, bf16[256,512]{1,0:T(8,128)(2,1)}, bf16[1024,256]{1,0:T(8,128)(2,1)}, bf16[256,2...) custom-call(f32[256,128]{1,0:T(8,128)} %get-tuple-element.18.points_r, ...), custom_call_target="tpu_custom_call" | custom-call | tf_op jit(solution)/shard_map/move/pallas_call | solution.py:482
  57.9 15.9 %tile.1 = (f32[1024,2048]{1,0:T(8,128)}, f32[1,1024]{1,0:T(1,128)}) custom-call(s32[5]{0:T(128)} %stack.27.info, f32[1024,2048]{1,0:T(8,128)} %prec_ref.1, bf16[1024,512]{1,0:T(8,128)(2,1)} %get-tuple-element.23.feat_r_ref, bf16[2048,512]{1,0:T(8,128)(2,1)} %get-tuple-element.24.feat_c_ref, bf16[256,512]{1,0:T(8,128)(2,1)} %get-tuple-element.25.feat_p_ref, ...), custom_call_target="tpu_custom_call" | custom-call | tf_op jit(solution)/shard_map/tile/pallas_call | solution.py:524
